TPU v7x, 256 devices: a whole 4x4x8 slice. The times are simulated.
256 devices in a mesh: row: 8 (over z_lo, y), col: 4 (over z_hi), depth: 8 (over x, core).
Axes of the slice: x: 4, y: 4, z: 8 (z_hi: 4, z_lo: 2; z = z_hi * 2 + z_lo), core: 2. Of those that a mesh axis runs over, the one named last changes fastest.
Arguments:
- tokens: bfloat16 [2048, 12288], P(('row', 'col'), 'depth'), may hold values from -6 to 6
- weight: bfloat16 [12288, 24576], P('depth', ('row', 'col')), may hold values from -5 to 5
- moment: bfloat16 [12288, 24576], P('depth', ('row', 'col')), may hold values from -0.59765625 to 0.59765625
- upstream: bfloat16 [8, 256, 24576], P(None, 'col', ('row', 'depth')), may hold values from -24 to 24
Outputs:
- activated: bfloat16 [8, 256, 24576], P(None, 'col', ('row', 'depth'))
- new_weight: bfloat16 [12288, 24576], P('depth', ('row', 'col'))
- new_moment: bfloat16 [12288, 24576], P('depth', ('row', 'col'))
All inputs are finite; a program needn't handle non-finite values.
Results may differ from a plain program's by a relative error of at most 0.015.
Values may be sent and summed in bfloat16 or wider, within the bound.
A program may use at most 64 MiB of HBM per device.

v0:
```python
import jax
import jax.numpy as jnp
from jax import lax
from jax.sharding import PartitionSpec as P

D = 12288
gelu_coef = 0.7978845608028654
cubic_coef = 0.044715
lion_rate = 0.5
decay_rate = 0.1
beta_one = 0.9
beta_two = 0.99
smooth_tau = 0.1


def gelu_pair(preact):
    tangent = jnp.tanh(gelu_coef * (preact + cubic_coef * preact * preact * preact))
    gelu_value = 0.5 * preact * (1.0 + tangent)
    gelu_slope = 0.5 * (1.0 + tangent) + 0.5 * preact * (1.0 - tangent * tangent) * gelu_coef * (
        1.0 + 3.0 * cubic_coef * preact * preact
    )
    return (gelu_value, gelu_slope)


def shards(tokens, weight, moment, upstream):
    row_count = lax.axis_size("row")
    tok_rows = tokens.shape[0]
    fan_scale = D ** (-0.5)
    gathered = lax.all_gather(tokens, "row", axis=0, tiled=True)
    partial_value = jnp.dot(
        gathered,
        lax.all_gather(weight, "col", axis=1, tiled=True),
        preferred_element_type=jnp.float32,
    )
    summed = lax.psum_scatter(
        partial_value.astype(jnp.bfloat16), "depth", scatter_dimension=1, tiled=True
    ).astype(jnp.float32)
    gelu_value, gelu_slope = gelu_pair(summed * fan_scale)
    activated = gelu_value.astype(jnp.bfloat16)
    upstream_flat = upstream.reshape(row_count * tok_rows, upstream.shape[2]).astype(jnp.float32)
    local_grad = (upstream_flat * gelu_slope).astype(jnp.bfloat16)
    act_grad = lax.all_gather(local_grad, "depth", axis=1, tiled=True)
    grad_panel = lax.dot_general(
        gathered, act_grad, (((0,), (0,)), ((), ())), preferred_element_type=jnp.float32
    )
    grad_sum = lax.psum_scatter(
        grad_panel.astype(jnp.bfloat16), "col", scatter_dimension=1, tiled=True
    ).astype(jnp.float32)
    grad_full = grad_sum * fan_scale
    moment_f = moment.astype(jnp.float32)
    weight_f = weight.astype(jnp.float32)
    blended = beta_one * moment_f + (1.0 - beta_one) * grad_full
    update = blended / jnp.sqrt(blended * blended + smooth_tau * smooth_tau)
    new_weight = (weight_f - lion_rate * (update + decay_rate * weight_f)).astype(jnp.bfloat16)
    new_moment = (beta_two * moment_f + (1.0 - beta_two) * grad_full).astype(jnp.bfloat16)
    activated = activated.reshape(upstream.shape[0], upstream.shape[1], activated.shape[1])
    return (activated, new_weight, new_moment)


def solution(mesh):
    placed = (
        P(("row", "col"), "depth"),
        P("depth", ("row", "col")),
        P("depth", ("row", "col")),
        P(None, "col", ("row", "depth")),
    )
    return jax.shard_map(
        shards,
        mesh=mesh,
        in_specs=placed,
        out_specs=(
            P(None, "col", ("row", "depth")),
            P("depth", ("row", "col")),
            P("depth", ("row", "col")),
        ),
        check_vma=False,
    )
```

profile of v0, /device:TPU:2, one launch (start us, length us, event | category | flops | bytes accessed | tf_op | source)
XLA Modules:
  0.0 509.9 jit_solution(10022676626198729526)
XLA Ops:
  7.2 0.0 all-gather.4.cloned.1.call-start
  7.2 0.7 all-gather.4.cloned.1.call-update
  7.9 0.0 all-gather.6.cloned.1.call-start
  7.9 0.7 all-gather.6.cloned.1.call-update
  8.6 0.0 reduce-scatter.7.cloned.1.call-start
  8.7 47.2 %all-gather.4.cloned.1.call-done = bf16[512,1536]{1,0:T(8,128)(2,1)} async-done(((bf16[64,1536]{1,0:T(8,128)(2,1)}), bf16[512,1536]{1,0:T(8,128)(2,1)}) %all-gather.4.cloned.1.call-update) | async-done | bytes 1572880 | tf_op jit(solution)/shard_map/all_gather | solution.py:29
  55.9 173.9 %all-gather.6.cloned.1.call-done = bf16[1536,3072]{1,0:T(8,128)(2,1)} async-done(((bf16[1536,768]{1,0:T(8,128)(2,1)}), bf16[1536,3072]{1,0:T(8,128)(2,1)}) %all-gather.6.cloned.1.call-update) | async-done | bytes 9437200 | tf_op jit(solution)/shard_map/all_gather | solution.py:32
  229.8 8.1 %convolution_convert_fusion.1 = bf16[512,3072]{1,0:T(8,128)(2,1)S(1)} fusion(bf16[512,1536]{1,0:T(8,128)(2,1)} %all-gather.4.cloned.1.call-done, bf16[1536,3072]{1,0:T(8,128)(2,1)} %all-gather.6.cloned.1.call-done), kind=kOutput, calls=%fused_computation.14 | convolution fusion | flops 4833411072 | bytes 14155776 | tf_op jit(solution)/shard_map/dot_general | solution.py:30
  237.9 0.0 copy-start.3
  237.9 2.8 copy.15
  240.7 0.0 copy-start.4
  240.7 0.0 reduce-scatter.7.cloned.1.call-update
  240.8 0.0 all-gather.8.cloned.1.call-start
  240.8 33.4 %reduce-scatter.7.cloned.1.call-done = bf16[384,512]{1,0:T(8,128)(2,1)} async-done(((bf16[3072,512]{1,0:T(8,128)(2,1)}), bf16[384,512]{1,0:T(8,128)(2,1)}) %reduce-scatter.7.cloned.1.call-update) | async-done | bytes 393232
  274.2 1.2 copy.16
  275.4 0.0 copy-done.3
  275.4 1.5 fusion.18
  277.0 0.0 all-gather.8.cloned.1.call-update
  277.0 0.0 reduce-scatter.5.cloned.1.call-start
  277.0 31.8 %all-gather.8.cloned.1.call-done = bf16[512,3072]{1,0:T(8,128)(2,1)} async-done(((bf16[512,384]{1,0:T(8,128)(2,1)}), bf16[512,3072]{1,0:T(8,128)(2,1)}) %all-gather.8.cloned.1.call-update) | async-done | bytes 3145744 | tf_op jit(solution)/shard_map/all_gather | solution.py:42
  308.8 0.0 copy-done.4
  308.8 9.6 %fusion = bf16[1536,3072]{0,1:T(8,128)(2,1)} fusion(bf16[512,3072]{1,0:T(8,128)(2,1)} %all-gather.8.cloned.1.call-done, bf16[512,1536]{1,0:T(8,128)(2,1)S(1)} %copy-done.4), kind=kOutput, calls=%fused_computation.1 | convolution fusion | flops 4836556800 | bytes 14155776 | tf_op jit(solution)/shard_map/dot_general | solution.py:43
  318.4 0.0 reduce-scatter.5.cloned.1.call-update
  318.4 1.6 copy-done
  320.1 2.4 copy.11
  322.5 4.4 copy.12
  326.9 163.8 %reduce-scatter.5.cloned.1.call-done = bf16[1536,768]{0,1:T(8,128)(2,1)} async-done(((bf16[1536,3072]{0,1:T(8,128)(2,1)}), bf16[1536,768]{0,1:T(8,128)(2,1)}) %reduce-scatter.5.cloned.1.call-update) | async-done | bytes 2359312 | tf_op jit(solution)/shard_map/reduce_scatter | solution.py:46
  490.7 0.0 copy-done.1
  490.7 5.9 %fusion.6 = (bf16[1536,768]{0,1:T(8,128)(2,1)}, bf16[1536,768]{0,1:T(8,128)(2,1)}) fusion(bf16[1536,768]{0,1:T(8,128)(2,1)} %copy.12, bf16[1536,768]{0,1:T(8,128)(2,1)} %reduce-scatter.5.cloned.1.call-done, bf16[1536,768]{0,1:T(8,128)(2,1)S(1)} %copy-done.1), kind=kLoop, calls=%fused_computation.13 | loop fusion | flops 21233664 | bytes 11796480 | tf_op jit(solution)/shard_map/convert_element_type | solution.py:55
  496.6 4.4 copy.13
  501.0 0.0 copy-done.2
  501.0 2.4 copy.14
  (3 shorter events, 0.0 us)
Async XLA Ops:
  7.2 48.8 %all-gather.4.cloned.1.call-start = ((), (), s32[]{:S(2)}) async-start(), calls=%async_computation.2 | async-start | bytes 1769472 | tf_op jit(solution)/shard_map/all_gather | solution.py:29
  7.9 221.9 %all-gather.6.cloned.1.call-start = ((), (), s32[]{:S(2)}) async-start(), calls=%async_computation.3 | async-start | bytes 11796480 | tf_op jit(solution)/shard_map/all_gather | solution.py:32
  8.6 265.6 %reduce-scatter.7.cloned.1.call-start = ((), (), s32[]{:S(2)}) async-start(), calls=%async_computation.6 | async-start | bytes 3538944
  237.9 37.5 %copy-start.3 = (bf16[8,64,384]{2,1,0:T(8,128)(2,1)S(1)}, bf16[8,64,384]{2,1,0:T(8,128)(2,1)}, u32[]{:S(2)}) copy-start(bf16[8,64,384]{2,1,0:T(8,128)(2,1)} %param.7) | copy-start | bytes 1179652
  240.7 68.1 %copy-start.4 = (bf16[512,1536]{1,0:T(8,128)(2,1)S(1)}, bf16[512,1536]{1,0:T(8,128)(2,1)}, u32[]{:S(2)}) copy-start(bf16[512,1536]{1,0:T(8,128)(2,1)} %all-gather.4.cloned.1.call-done) | copy-start | bytes 4718596
  240.8 68.0 %all-gather.8.cloned.1.call-start = ((), (), s32[]{:S(2)}) async-start(), calls=%async_computation.4 | async-start | bytes 3538944 | tf_op jit(solution)/shard_map/all_gather | solution.py:42
  277.0 213.7 %reduce-scatter.5.cloned.1.call-start = ((), (), s32[]{:S(2)}) async-start(), calls=%async_computation.5 | async-start | bytes 11796480 | tf_op jit(solution)/shard_map/reduce_scatter | solution.py:46
  318.4 1.7 copy-start
  322.5 168.2 %copy-start.1 = (bf16[1536,768]{0,1:T(8,128)(2,1)S(1)}, bf16[1536,768]{0,1:T(8,128)(2,1)}, u32[]{:S(2)}) copy-start(bf16[1536,768]{0,1:T(8,128)(2,1)} %copy.11) | copy-start | bytes 7077892
  496.6 4.4 copy-start.2
Sparse Core Ops, SparseCore 0:
  9.8 46.0 all-gather.3
  57.7 172.0 all-gather.5
  240.9 33.2 reduce-scatter.6
  277.1 31.6 all-gather.7
  318.5 172.1 reduce-scatter.4
where the time goes:
time: 510 us
  waiting for transfers between devices  452 us (89%)
  local copies, waits for them, and re-layouts  19.4 us (4%)
  matrix products  17.7 us (3%)
  between operations  13.8 us (3%)
  other arithmetic  7.4 us (1%)
    all_gather x1, waiting for transfers between devices, shards(): lax.all_gather(weight, 'col', axis=1, tiled=True)  174 us
    reduce_scatter x1, waiting for transfers between devices, shards(): lax.psum_scatter(grad_panel.astype(jnp.bfloat16), 'col', scatter_dimensio...  164 us
    all_gather x1, waiting for transfers between devices, shards(): gathered = lax.all_gather(tokens, 'row', axis=0, tiled=True)  47.2 us
    unnamed x6, waiting for transfers between devices  34.8 us
    all_gather x1, waiting for transfers between devices, shards(): act_grad = lax.all_gather(local_grad, 'depth', axis=1, tiled=True)  31.8 us
    unnamed x16, local copies, waits for them, and re-layouts  19.4 us
  transfers between devices with their start and end apart: 5, of which 5 were waited for; matrix products, arithmetic and copies ran while one was open for 1% of the time, Pallas kernels for 0%

commit v1 on v0

--- a/solution.py
+++ b/solution.py
@@ -11,6 +11,30 @@
 beta_one = 0.9
 beta_two = 0.99
 smooth_tau = 0.1
+
+
+def part_the_trees(content, array_axis):
+    shaped = list(content.shape[1:])
+    shaped[array_axis] *= content.shape[0]
+    return jnp.moveaxis(content, 0, array_axis).reshape(shaped)
+
+
+def name_slot(incoming_x, named_axis):
+    state_next, tmp = (lax.axis_size(named_axis), lax.axis_index(named_axis))
+    upper, reply = (incoming_x[None], 1)
+    while reply < state_next:
+        later = lax.ppermute(
+            upper, axis_name=named_axis, perm=[(ii, ii ^ reply) for ii in range(state_next)]
+        )
+        g_now = tmp & reply == 0
+        upper = jnp.concatenate([jnp.where(g_now, upper, later), jnp.where(g_now, later, upper)])
+        reply *= 2
+    return upper
+
+
+def draft_slabs_on_mesh(frame_in, message, dim_i):
+    val = name_slot(frame_in, message)
+    return part_the_trees(val, dim_i)
 
 
 def gelu_pair(preact):
@@ -39,7 +63,7 @@
     activated = gelu_value.astype(jnp.bfloat16)
     upstream_flat = upstream.reshape(row_count * tok_rows, upstream.shape[2]).astype(jnp.float32)
     local_grad = (upstream_flat * gelu_slope).astype(jnp.bfloat16)
-    act_grad = lax.all_gather(local_grad, "depth", axis=1, tiled=True)
+    act_grad = draft_slabs_on_mesh(local_grad, "depth", 1)
     grad_panel = lax.dot_general(
         gathered, act_grad, (((0,), (0,)), ((), ())), preferred_element_type=jnp.float32
     )

time: 510 us -> 544 us (1.067)
  waiting for transfers between devices: 452 us -> 473 us
  starting transfers between devices: 0.2 us -> 5.81 us
    ppermute x0 -> x3, waiting for transfers between devices: none -> 55.6 us  [name_slot(): lax.ppermute(upper, axis_name=named_axis, perm=[(ii, ii ^ reply) for ii i...]
    all_gather x1 -> x0, waiting for transfers between devices: 31.8 us -> none  [shards(): act_grad = lax.all_gather(local_grad, 'depth', axis=1, tiled=True)]
    ppermute x0 -> x3, starting transfers between devices: none -> 5.66 us  [name_slot(): lax.ppermute(upper, axis_name=named_axis, perm=[(ii, ii ^ reply) for ii i...]
    unnamed x6 -> x5, waiting for transfers between devices: 34.8 us -> 34.8 us
    unnamed x16 -> x14, local copies, waits for them, and re-layouts: 19.4 us -> 19.4 us
  transfers between devices with their start and end apart: 5 -> 7, of which waited for: 5 -> 7; matrix products, arithmetic and copies ran while one was open for 1% -> 1% of each run, Pallas kernels for 0% -> 0%
where the time goes in v1:
time: 544 us; the launch traced here: 542 us
  waiting for transfers between devices  473 us (87%)
  local copies, waits for them, and re-layouts  22.2 us (4%)
  matrix products  17.4 us (3%)
  between operations  13.8 us (3%)
  other arithmetic  9.97 us (2%)
  starting transfers between devices  5.81 us (1%)
    all_gather x1, waiting for transfers between devices, shards(): lax.all_gather(weight, 'col', axis=1, tiled=True)  174 us
    reduce_scatter x1, waiting for transfers between devices, shards(): lax.psum_scatter(grad_panel.astype(jnp.bfloat16), 'col', scatter_dimensio...  161 us
    ppermute x3, waiting for transfers between devices, name_slot(): lax.ppermute(upper, axis_name=named_axis, perm=[(ii, ii ^ reply) for ii i...  55.6 us
    all_gather x1, waiting for transfers between devices, shards(): gathered = lax.all_gather(tokens, 'row', axis=0, tiled=True)  47.2 us
    unnamed x5, waiting for transfers between devices  34.8 us
    unnamed x14, local copies, waits for them, and re-layouts  19.4 us
  transfers between devices with their start and end apart: 7, of which 7 were waited for; matrix products, arithmetic and copies ran while one was open for 1% of the time, Pallas kernels for 0%

profile of v1, /device:TPU:2, one launch (start us, length us, event | category | flops | bytes accessed | tf_op | source)
XLA Modules:
  0.0 542.1 jit_solution(12554795887554093073)
XLA Ops:
  7.2 0.7 all-gather.3.cloned.1.call-update
  7.9 0.0 all-gather.5.cloned.1.call-start
  7.9 0.7 all-gather.5.cloned.1.call-update
  8.6 0.0 reduce-scatter.7.cloned.1.call-start
  8.7 47.2 %all-gather.3.cloned.1.call-done = bf16[512,1536]{1,0:T(8,128)(2,1)} async-done(((bf16[64,1536]{1,0:T(8,128)(2,1)}), bf16[512,1536]{1,0:T(8,128)(2,1)}) %all-gather.3.cloned.1.call-update) | async-done | bytes 1572880 | tf_op jit(solution)/shard_map/all_gather | solution.py:53
  55.9 173.9 %all-gather.5.cloned.1.call-done = bf16[1536,3072]{1,0:T(8,128)(2,1)} async-done(((bf16[1536,768]{1,0:T(8,128)(2,1)}), bf16[1536,3072]{1,0:T(8,128)(2,1)}) %all-gather.5.cloned.1.call-update) | async-done | bytes 9437200 | tf_op jit(solution)/shard_map/all_gather | solution.py:56
  229.8 8.1 %convolution_convert_fusion.1 = bf16[512,3072]{1,0:T(8,128)(2,1)S(1)} fusion(bf16[512,1536]{1,0:T(8,128)(2,1)} %all-gather.3.cloned.1.call-done, bf16[1536,3072]{1,0:T(8,128)(2,1)} %all-gather.5.cloned.1.call-done), kind=kOutput, calls=%fused_computation.14 | convolution fusion | flops 4833411072 | bytes 14155776 | tf_op jit(solution)/shard_map/dot_general | solution.py:54
  237.9 2.8 copy.28
  240.8 0.0 reduce-scatter.5.cloned.1.call-start
  240.8 33.4 %reduce-scatter.7.cloned.1.call-done = bf16[384,512]{1,0:T(8,128)(2,1)} async-done(((bf16[3072,512]{1,0:T(8,128)(2,1)}), bf16[384,512]{1,0:T(8,128)(2,1)}) %reduce-scatter.7.cloned.1.call-update) | async-done | bytes 393232
  274.2 1.2 copy.29
  275.4 1.4 fusion.18
  276.8 1.7 collective-permute-done
  278.6 0.1 broadcast_select_fusion.5
  278.6 0.1 pad_maximum_fusion.1
  278.7 4.0 collective-permute-start.1
  282.8 17.8 %collective-permute-done.1 = bf16[2,512,384]{2,1,0:T(8,128)(2,1)S(1)} collective-permute-done((bf16[2,512,384]{2,1,0:T(8,128)(2,1)S(1)}, bf16[2,512,384]{2,1,0:T(8,128)(2,1)S(1)}, u32[]{:S(2)}, u32[]{:S(2)}) %collective-permute-start.1) | collective-permute-done | bytes 786464 | tf_op jit(solution)/shard_map/ppermute | solution.py:26
  300.6 0.2 broadcast_select_fusion.3
  300.8 0.2 pad_maximum_fusion
  301.0 1.6 collective-permute-start.2
  302.6 36.0 %collective-permute-done.2 = bf16[4,512,384]{2,1,0:T(8,128)(2,1)} collective-permute-done((bf16[4,512,384]{2,1,0:T(8,128)(2,1)S(1)}, bf16[4,512,384]{2,1,0:T(8,128)(2,1)}, u32[]{:S(2)}, u32[]{:S(2)}) %collective-permute-start.2) | collective-permute-done | bytes 1572896 | tf_op jit(solution)/shard_map/ppermute | solution.py:26
  338.6 1.8 broadcast_select_fusion.1
  340.4 0.4 maximum_bitcast_fusion
  340.8 2.9 copy.25
  343.7 9.3 %fusion = bf16[1536,3072]{0,1:T(8,128)(2,1)} fusion(bf16[512,3072]{0,1:T(8,128)(2,1)} %bitcast.19, bf16[512,1536]{1,0:T(8,128)(2,1)} %all-gather.3.cloned.1.call-done), kind=kOutput, calls=%fused_computation.1 | convolution fusion | flops 4836556800 | bytes 14155776 | tf_op jit(solution)/shard_map/dot_general | solution.py:67
  353.0 1.6 copy-done
  354.6 2.4 copy.23
  357.1 4.4 copy.24
  361.5 161.4 %reduce-scatter.5.cloned.1.call-done = bf16[1536,768]{0,1:T(8,128)(2,1)} async-done(((bf16[1536,3072]{0,1:T(8,128)(2,1)}), bf16[1536,768]{0,1:T(8,128)(2,1)}) %reduce-scatter.5.cloned.1.call-update) | async-done | bytes 2359312 | tf_op jit(solution)/shard_map/reduce_scatter | solution.py:70
  522.9 5.8 %fusion.6 = (bf16[1536,768]{0,1:T(8,128)(2,1)}, bf16[1536,768]{0,1:T(8,128)(2,1)}) fusion(bf16[1536,768]{0,1:T(8,128)(2,1)} %copy.24, bf16[1536,768]{0,1:T(8,128)(2,1)} %reduce-scatter.5.cloned.1.call-done, bf16[1536,768]{0,1:T(8,128)(2,1)S(1)} %copy-done.1), kind=kLoop, calls=%fused_computation.13 | loop fusion | flops 21233664 | bytes 11796480 | tf_op jit(solution)/shard_map/convert_element_type | solution.py:79
  528.7 4.4 copy.26
  533.2 2.4 copy.27
  (11 shorter events, 0.1 us)
Async XLA Ops:
  7.2 48.8 %all-gather.3.cloned.1.call-start = ((), (), s32[]{:S(2)}) async-start(), calls=%async_computation.2 | async-start | bytes 1769472 | tf_op jit(solution)/shard_map/all_gather | solution.py:53
  7.9 221.9 %all-gather.5.cloned.1.call-start = ((), (), s32[]{:S(2)}) async-start(), calls=%async_computation.3 | async-start | bytes 11796480 | tf_op jit(solution)/shard_map/all_gather | solution.py:56
  8.6 265.6 %reduce-scatter.7.cloned.1.call-start = ((), (), s32[]{:S(2)}) async-start(), calls=%async_computation.5 | async-start | bytes 3538944
  240.7 34.7 %copy-start.3 = (bf16[8,64,384]{2,1,0:T(8,128)(2,1)S(1)}, bf16[8,64,384]{2,1,0:T(8,128)(2,1)}, u32[]{:S(2)}) copy-start(bf16[8,64,384]{2,1,0:T(8,128)(2,1)} %param.7) | copy-start | bytes 1179652
  240.8 282.1 %reduce-scatter.5.cloned.1.call-start = ((), (), s32[]{:S(2)}) async-start(), calls=%async_computation.4 | async-start | bytes 11796480 | tf_op jit(solution)/shard_map/reduce_scatter | solution.py:70
  276.8 1.7 collective-permute-start
  278.7 21.9 %collective-permute-start.1 = (bf16[2,512,384]{2,1,0:T(8,128)(2,1)S(1)}, bf16[2,512,384]{2,1,0:T(8,128)(2,1)S(1)}, u32[]{:S(2)}, u32[]{:S(2)}) collective-permute-start(bf16[2,512,384]{2,1,0:T(8,128)(2,1)S(1)} %pad_maximum_fusion.1), channel_id=1, source_target_pairs={{0,2},{1,3},{2,0},{3,1},{4,6},{5,7},{6,4},{7,5},{8,10},{9,11},{10,... | collective-permute-start | bytes 2359304 | tf_op jit(solution)/shard_map/ppermute | solution.py:26
  301.0 37.6 %collective-permute-start.2 = (bf16[4,512,384]{2,1,0:T(8,128)(2,1)S(1)}, bf16[4,512,384]{2,1,0:T(8,128)(2,1)}, u32[]{:S(2)}, u32[]{:S(2)}) collective-permute-start(bf16[4,512,384]{2,1,0:T(8,128)(2,1)S(1)} %pad_maximum_fusion), channel_id=1, source_target_pairs={{0,4},{1,5},{2,6},{3,7},{4,0},{5,1},{6,2},{7,3},{8,12},{9,13},{10,... | collective-permute-start | bytes 4718600 | tf_op jit(solution)/shard_map/ppermute | solution.py:26
  353.0 1.7 copy-start
  357.1 165.8 %copy-start.1 = (bf16[1536,768]{0,1:T(8,128)(2,1)S(1)}, bf16[1536,768]{0,1:T(8,128)(2,1)}, u32[]{:S(2)}) copy-start(bf16[1536,768]{0,1:T(8,128)(2,1)} %copy.23) | copy-start | bytes 7077892
  528.7 4.4 copy-start.2
Sparse Core Ops, SparseCore 0:
  9.8 46.0 all-gather.2
  57.7 172.0 all-gather.4
  240.9 33.2 reduce-scatter.6
  353.1 169.7 reduce-scatter.4
